TPU v7x, 32 devices: a whole 2x2x4 slice. The times are simulated.
32 devices in a mesh: rep: 2 (over y), cell: 4 (over z), scen: 4 (over x, core).
Axes of the slice: x: 2, y: 2, z: 4, core: 2. Of those that a mesh axis runs over, the one named last changes fastest.
Arguments:
- hydrograph: bfloat16 [1024, 128], P(('rep', 'scen')), parts along dimension 0, may hold values from -6 to 6
- scen_group: int32 [1024], P(('rep', 'scen')), parts along dimension 0, may hold values from 0 to 15
- cell_feat: bfloat16 [4096, 128], P(('rep', 'cell')), parts along dimension 0, may hold values from -6 to 6
- cell_class: int32 [32], P(('rep', 'cell')), parts along dimension 0, may hold values from 0 to 15
- branch_in: bfloat16 [128, 1024], replicated, may hold values from -0.5 to 0.5
- group_table: bfloat16 [16, 1024], replicated, may hold values from -3 to 3
- branch_out: bfloat16 [1024, 512], replicated, may hold values from -0.1875 to 0.1875
- trunk_in: bfloat16 [128, 512], replicated, may hold values from -0.5 to 0.5
- class_table: bfloat16 [16, 512], replicated, may hold values from -3 to 3
- trunk_out: bfloat16 [512, 512], replicated, may hold values from -0.25 to 0.25
- targets: float32 [1024, 2048], P(('rep', 'scen'), 'cell'), parts along dimension 0, may hold values from -6 to 6
Outputs:
- gradient: float32 [2015232], P(('rep', 'cell', 'scen')), parts along dimension 0
There are 2 independent parts, one for each index of `rep`. A program takes and returns all parts, laid end to end along the dimension named above; an argument that names none is the same for every part. Nothing has to cross between parts.
All inputs are finite; a program needn't handle non-finite values.
Results may differ from a plain program's by a relative error of at most 0.0034.
Values may be sent and summed in bfloat16 or wider, within the bound.
A program may use at most 64 MiB of HBM per device.

v0:
```python
import jax
import jax.numpy as jnp
from jax import lax
from jax.sharding import PartitionSpec as P


def contract(left, right, left_dim, right_dim):
    return lax.dot_general(
        left, right, (((left_dim,), (right_dim,)), ((), ())), preferred_element_type=jnp.float32
    )


def reduce_whole(flat_terms):
    return lax.psum_scatter(flat_terms, ("cell", "scen"), scatter_dimension=0, tiled=True)


def shards(
    hydrograph,
    scen_group,
    cell_feat,
    cell_class,
    branch_in,
    group_table,
    branch_out,
    trunk_in,
    class_table,
    trunk_out,
    targets,
):
    cell_count = lax.axis_size("cell")
    scen_count = lax.axis_size("scen")
    scen_rows = hydrograph.shape[0]
    cell_rows = cell_feat.shape[0]
    basis_width = branch_out.shape[1]
    group_count = group_table.shape[0]
    class_count = class_table.shape[0]
    whole_pairs = jnp.float32(scen_rows * scen_count) * jnp.float32(cell_rows * cell_count)
    group_hot = (scen_group[:, None] == jnp.arange(group_count, dtype=jnp.int32)[None, :]).astype(
        jnp.bfloat16
    )
    class_cells = jnp.repeat(cell_class, 128)
    class_hot = (class_cells[:, None] == jnp.arange(class_count, dtype=jnp.int32)[None, :]).astype(
        jnp.bfloat16
    )
    pre_branch = jnp.dot(hydrograph, branch_in, preferred_element_type=jnp.float32) + jnp.dot(
        group_hot, group_table, preferred_element_type=jnp.float32
    )
    hid_branch = jax.nn.gelu(pre_branch).astype(jnp.bfloat16)
    coeff_local = jnp.dot(hid_branch, branch_out, preferred_element_type=jnp.float32).astype(
        jnp.bfloat16
    )
    pre_trunk = jnp.dot(cell_feat, trunk_in, preferred_element_type=jnp.float32) + jnp.dot(
        class_hot, class_table, preferred_element_type=jnp.float32
    )
    hid_trunk = jnp.tanh(pre_trunk).astype(jnp.bfloat16)
    basis_local = jnp.dot(hid_trunk, trunk_out, preferred_element_type=jnp.float32).astype(
        jnp.bfloat16
    )
    predicted = contract(coeff_local, basis_local, 1, 1) * (
        1.0 / jnp.sqrt(jnp.float32(basis_width))
    )
    resid = ((predicted - targets) * (1.0 / jnp.sqrt(whole_pairs))).astype(jnp.bfloat16)
    d_coeff = lax.psum(
        jnp.dot(resid, basis_local, preferred_element_type=jnp.float32), "cell"
    ).astype(jnp.bfloat16)
    d_basis = lax.psum(contract(resid, coeff_local, 0, 0).astype(jnp.bfloat16), "scen")
    g_branch_out = contract(hid_branch, d_coeff, 0, 0)
    d_hid_branch = contract(d_coeff, branch_out, 1, 1)
    d_pre_branch = jax.vjp(jax.nn.gelu, pre_branch)[1](d_hid_branch)[0].astype(jnp.bfloat16)
    g_branch_in = contract(hydrograph, d_pre_branch, 0, 0)
    g_group_table = contract(group_hot, d_pre_branch, 0, 0)
    g_trunk_out = contract(hid_trunk, d_basis, 0, 0)
    d_hid_trunk = contract(d_basis, trunk_out, 1, 1)
    d_pre_trunk = jax.vjp(jnp.tanh, pre_trunk)[1](d_hid_trunk)[0].astype(jnp.bfloat16)
    g_trunk_in = contract(cell_feat, d_pre_trunk, 0, 0)
    g_class_table = contract(class_hot, d_pre_trunk, 0, 0)
    branch_flat = jnp.concatenate(
        [g_branch_in.ravel(), g_group_table.ravel(), g_branch_out.ravel()]
    )
    trunk_flat = jnp.concatenate([g_trunk_in.ravel(), g_class_table.ravel(), g_trunk_out.ravel()])
    branch_flat = branch_flat * (lax.axis_index("cell") == 0).astype(jnp.float32)
    trunk_flat = trunk_flat * (lax.axis_index("scen") == 0).astype(jnp.float32)
    flat_grad = jnp.concatenate([branch_flat, trunk_flat])
    return reduce_whole(flat_grad)


def solution(mesh):
    in_specs = (
        P(("rep", "scen"), None),
        P(("rep", "scen")),
        P(("rep", "cell"), None),
        P(("rep", "cell")),
        P(),
        P(),
        P(),
        P(),
        P(),
        P(),
        P(("rep", "scen"), "cell"),
    )
    out_specs = P(("rep", "cell", "scen"))
    return jax.shard_map(shards, mesh=mesh, in_specs=in_specs, out_specs=out_specs, check_vma=False)
```

profile of v0, /device:TPU:1, one launch (start us, length us, event | category | flops | bytes accessed | tf_op | source)
XLA Modules:
  0.0 175.8 jit_solution(13507408094021599108)
XLA Ops:
  6.5 0.0 copy-start
  6.5 0.0 copy-start.3
  6.5 0.0 all-reduce.5.cloned.1.call-start
  6.5 0.8 broadcast_bitcast_fusion
  7.4 0.0 copy-start.7
  7.4 0.0 copy-start.9
  7.4 1.3 fusion.24
  8.7 0.0 copy-start.10
  8.7 0.0 copy-start.11
  8.7 1.1 fusion
  9.8 0.0 copy-done.3
  9.8 0.0 copy-start.8
  9.8 0.4 convolution_convert_fusion
  10.3 0.0 copy-done.7
  10.3 0.0 copy-done.9
  10.3 0.2 fusion.23
  10.5 0.0 copy-done.10
  10.5 0.0 copy-done.11
  10.5 0.3 convolution_add_fusion.1
  10.8 0.0 copy-start.4
  10.8 0.8 copy-done.4
  11.6 0.0 copy-done
  11.6 0.4 convolution_convert_fusion.2
  12.0 0.0 copy-done.8
  12.0 0.3 fusion.4
  12.3 1.2 convolution_convert_fusion.1
  13.4 0.0 all-reduce.5.cloned.1.call-update
  13.5 0.0 all-reduce.7.cloned.1.call-start
  13.5 0.2 fusion.25
  13.7 20.6 %all-reduce.8 = bf16[128,512]{1,0:T(8,128)(2,1)S(1)} all-reduce(f32[128,512]{1,0:T(8,128)S(1)} %fusion.25), channel_id=1, replica_groups=mesh['rep'=2,'cell'=4,'scen'=4] {'cell'}, use_global_device_ids=true, to_apply=%region_0.0 | all-reduce | flops 65536 | bytes 393216 | tf_op jit(solution)/shard_map/psum | solution.py:63
  34.3 0.0 copy-start.5
  34.3 1.7 fusion.11
  36.1 1.0 convolution_bitcast_fusion.2
  37.1 0.3 convolution_bitcast_fusion.4
  37.3 0.0 copy-done.5
  37.3 1.8 %convolution_bitcast_fusion = f32[128,4,8,128]{3,2,1,0:T(8,128)} fusion(bf16[128,512]{1,0:T(8,128)(2,1)S(1)} %all-reduce.8, f32[128,1024]{1,0:T(8,128)S(1)} %copy-done.5), kind=kOutput, calls=%fused_computation.2 | convolution fusion | flops 135397376 | bytes 2752512 | tf_op jit(solution)/shard_map/dot_general | solution.py:8
  39.2 1.0 copy.14
  40.2 1.1 copy.16
  41.4 3.5 %copy.18 = f32[128,4,8,128]{3,1,2,0:T(4,128)} copy(f32[128,4,8,128]{3,2,1,0:T(8,128)} %convolution_bitcast_fusion) | data formatting | bytes 4194304
  44.8 3.3 %maximum_multiply_fusion = f32[671744]{0:T(1024)} fusion(f32[524288]{0:T(1024)} %bitcast.49, f32[16384]{0:T(1024)S(1)} %bitcast.55, f32[131072]{0:T(1024)S(1)} %bitcast.52, f32[]{:T(128)S(6)} %convert_element_type.42), kind=kLoop, calls=%fused_computation.1 | loop fusion | flops 2015232 | bytes 5373956 | tf_op jit(solution)/shard_map/mul | solution.py:81
  48.1 0.0 copy-start.6
  48.1 0.0 all-reduce.5.cloned.1.call-done
  48.1 0.0 copy-start.2
  48.1 1.6 fusion.1
  49.7 0.3 convolution_bitcast_fusion.5
  50.0 0.0 copy-done.6
  50.0 0.3 convolution_bitcast_fusion.3
  50.4 0.1 copy.15
  50.5 0.1 copy.19
  50.6 0.0 copy-done.2
  50.6 0.5 convolution_bitcast_fusion.1
  51.1 0.0 copy-start.1
  51.1 0.3 copy.21
  51.4 0.1 maximum_multiply_fusion.1
  51.5 1.4 copy-done.1
  52.8 2.2 %pad_maximum_fusion = f32[1007616]{0:T(1024)} fusion(f32[335872]{0:T(1024)S(1)} %maximum_multiply_fusion.1, f32[671744]{0:T(1024)S(1)} %copy-done.1), kind=kLoop, calls=%fused_computation | loop fusion | flops 1007616 | bytes 8060928 | tf_op jit(solution)/shard_map/concatenate | solution.py:83
  55.0 0.0 copy-start.12
  55.0 0.0 all-reduce.7.cloned.1.call-update
  55.0 0.6 copy-done.12
  55.7 0.6 dynamic-slice
  56.9 110.2 %all-reduce.7.cloned.1.call-done = f32[1007616]{0:T(1024)} async-done(((f32[1007616]{0:T(1024)}), f32[1007616]{0:T(1024)}) %all-reduce.7.cloned.1.call-update) | async-done | bytes 4030480
  167.2 1.8 %dynamic-slice.1 = f32[62976]{0:T(1024)} dynamic-slice(f32[1007616]{0:T(1024)} %all-reduce.7.cloned.1.call-done, u32[]{:T(128)S(6)} %multiply.3), dynamic_slice_sizes={62976} | dynamic-slice | bytes 503812
  (2 shorter events, 0.0 us)
Async XLA Ops:
  6.5 5.1 %copy-start = (bf16[1024,512]{1,0:T(8,128)(2,1)S(1)}, bf16[1024,512]{1,0:T(8,128)(2,1)}, u32[]{:S(2)}) copy-start(bf16[1024,512]{1,0:T(8,128)(2,1)} %param.17) | copy-start | bytes 3145732
  6.5 3.3 %copy-start.3 = (bf16[512,512]{1,0:T(8,128)(2,1)S(1)}, bf16[512,512]{1,0:T(8,128)(2,1)}, u32[]{:S(2)}) copy-start(bf16[512,512]{1,0:T(8,128)(2,1)} %param.20) | copy-start | bytes 1572868
  6.5 41.6 %all-reduce.5.cloned.1.call-start = ((), (), s32[]{:S(2)}) async-start(), calls=%async_computation | async-start | bytes 1048576 | tf_op jit(solution)/shard_map/psum | solution.py:66
  7.4 2.9 %copy-start.7 = (bf16[128,1024]{1,0:T(8,128)(2,1)S(1)}, bf16[128,1024]{1,0:T(8,128)(2,1)}, u32[]{:S(2)}) copy-start(bf16[128,1024]{1,0:T(8,128)(2,1)} %param.15) | copy-start | bytes 786436
  7.4 2.9 %copy-start.9 = (bf16[128,128]{1,0:T(8,128)(2,1)S(1)}, bf16[128,128]{1,0:T(8,128)(2,1)}, u32[]{:S(2)}) copy-start(bf16[128,128]{1,0:T(8,128)(2,1)} %param.11) | copy-start | bytes 98308
  8.7 1.8 %copy-start.10 = (bf16[16,1024]{1,0:T(8,128)(2,1)S(1)}, bf16[16,1024]{1,0:T(8,128)(2,1)}, u32[]{:S(2)}) copy-start(bf16[16,1024]{1,0:T(8,128)(2,1)} %param.16) | copy-start | bytes 98308
  8.7 1.8 %copy-start.11 = (s32[128]{0:T(128)S(1)}, s32[128]{0:T(128)}, u32[]{:S(2)}) copy-start(s32[128]{0:T(128)} %param.12) | copy-start | bytes 1540
  9.8 2.2 %copy-start.8 = (f32[128,512]{1,0:T(8,128)S(1)}, f32[128,512]{1,0:T(8,128)}, u32[]{:S(2)}) copy-start(f32[128,512]{1,0:T(8,128)} %param.21) | copy-start | bytes 786436
  10.8 0.8 copy-start.4
  13.5 153.7 %all-reduce.7.cloned.1.call-start = ((), (), s32[]{:S(2)}) async-start(), calls=%async_computation.1 | async-start | bytes 8060928
  34.3 3.0 %copy-start.5 = (f32[128,1024]{1,0:T(8,128)S(1)}, f32[128,1024]{1,0:T(8,128)}, u32[]{:S(2)}) copy-start(f32[128,1024]{1,0:T(8,128)} %copy-done.4) | copy-start | bytes 1572868
  48.1 1.9 %copy-start.6 = (bf16[512,128]{1,0:T(8,128)(2,1)S(1)}, bf16[512,128]{1,0:T(8,128)(2,1)}, u32[]{:S(2)}) copy-start(bf16[512,128]{1,0:T(8,128)(2,1)} %param.13) | copy-start | bytes 393220
  48.1 2.5 %copy-start.2 = (bf16[512,512]{1,0:T(8,128)(2,1)S(1)}, bf16[512,512]{1,0:T(8,128)(2,1)}, u32[]{:S(2)}) copy-start(bf16[512,512]{1,0:T(8,128)(2,1)} %all-reduce.5.cloned.1.call-done) | copy-start | bytes 1572868
  51.1 1.8 %copy-start.1 = (f32[671744]{0:T(1024)S(1)}, f32[671744]{0:T(1024)}, u32[]{:S(2)}) copy-start(f32[671744]{0:T(1024)} %maximum_multiply_fusion) | copy-start | bytes 8060932
  55.0 0.7 copy-start.12
Sparse Core Ops, SparseCore 0:
  13.6 33.9 all-reduce.4
  55.2 111.9 all-reduce.6
where the time goes:
time: 178 us; the launch traced here: 176 us
  waiting for transfers between devices  110 us (62%)
  blocking collectives  20.6 us (12%)
  between operations  14.3 us (8%)
  matrix products  12.9 us (7%)
  local copies, waits for them, and re-layouts  12.1 us (7%)
  other arithmetic  5.56 us (3%)
    unnamed x3, waiting for transfers between devices  110 us
    psum x1, blocking collectives, shards(): lax.psum(jnp.dot(resid, basis_local, preferred_element_type=jnp.float32),...  20.6 us
    unnamed x34, local copies, waits for them, and re-layouts  10.2 us
    dot_general x10, matrix products, contract(): lax.dot_general(left, right, (((left_dim,), (right_dim,)), ((), ())), pre...  8.98 us
  transfers between devices with their start and end apart: 2, of which 1 were waited for; matrix products, arithmetic and copies ran while one was open for 8% of the time, Pallas kernels for 0%

commit v1 on v0

v1 whole, which is shorter than its diff:
```python
import math

import jax
import jax.numpy as jnp
from jax import lax
from jax.experimental import pallas as pl
from jax.experimental.pallas import tpu as pltpu
from jax.sharding import PartitionSpec as P

MESH = pl.DeviceIdType.MESH
BF16 = jnp.bfloat16
F32 = jnp.float32
WIDE = 512


def contract(left, right, left_dim, right_dim):
    return lax.dot_general(
        left, right, (((left_dim,), (right_dim,)), ((), ())), preferred_element_type=jnp.float32
    )


def plain_shards(
    hydrograph,
    scen_group,
    cell_feat,
    cell_class,
    branch_in,
    group_table,
    branch_out,
    trunk_in,
    class_table,
    trunk_out,
    targets,
):
    cell_count = lax.axis_size("cell")
    scen_count = lax.axis_size("scen")
    whole_pairs = jnp.float32(hydrograph.shape[0] * scen_count) * jnp.float32(
        cell_feat.shape[0] * cell_count
    )
    group_hot = (
        scen_group[:, None] == jnp.arange(group_table.shape[0], dtype=jnp.int32)[None, :]
    ).astype(BF16)
    class_cells = jnp.repeat(cell_class, 128)
    class_hot = (
        class_cells[:, None] == jnp.arange(class_table.shape[0], dtype=jnp.int32)[None, :]
    ).astype(BF16)
    pre_branch = contract(hydrograph, branch_in, 1, 0) + contract(group_hot, group_table, 1, 0)
    hid_branch = jax.nn.gelu(pre_branch).astype(BF16)
    coeff_local = contract(hid_branch, branch_out, 1, 0).astype(BF16)
    pre_trunk = contract(cell_feat, trunk_in, 1, 0) + contract(class_hot, class_table, 1, 0)
    hid_trunk = jnp.tanh(pre_trunk).astype(BF16)
    basis_local = contract(hid_trunk, trunk_out, 1, 0).astype(BF16)
    predicted = contract(coeff_local, basis_local, 1, 1) * (
        1.0 / jnp.sqrt(jnp.float32(branch_out.shape[1]))
    )
    resid = ((predicted - targets) * (1.0 / jnp.sqrt(whole_pairs))).astype(BF16)
    d_coeff = lax.psum(contract(resid, basis_local, 1, 0), "cell").astype(BF16)
    d_basis = lax.psum(contract(resid, coeff_local, 0, 0).astype(BF16), "scen")
    g_branch_out = contract(hid_branch, d_coeff, 0, 0)
    d_hid_branch = contract(d_coeff, branch_out, 1, 1)
    d_pre_branch = jax.vjp(jax.nn.gelu, pre_branch)[1](d_hid_branch)[0].astype(BF16)
    g_branch_in = contract(hydrograph, d_pre_branch, 0, 0)
    g_group_table = contract(group_hot, d_pre_branch, 0, 0)
    g_trunk_out = contract(hid_trunk, d_basis, 0, 0)
    d_hid_trunk = contract(d_basis, trunk_out, 1, 1)
    d_pre_trunk = jax.vjp(jnp.tanh, pre_trunk)[1](d_hid_trunk)[0].astype(BF16)
    g_trunk_in = contract(cell_feat, d_pre_trunk, 0, 0)
    g_class_table = contract(class_hot, d_pre_trunk, 0, 0)
    branch_flat = jnp.concatenate(
        [g_branch_in.ravel(), g_group_table.ravel(), g_branch_out.ravel()]
    )
    trunk_flat = jnp.concatenate([g_trunk_in.ravel(), g_class_table.ravel(), g_trunk_out.ravel()])
    branch_flat = branch_flat * (lax.axis_index("cell") == 0).astype(F32)
    trunk_flat = trunk_flat * (lax.axis_index("scen") == 0).astype(F32)
    flat_grad = jnp.concatenate([branch_flat, trunk_flat])
    return lax.psum_scatter(flat_grad, ("cell", "scen"), scatter_dimension=0, tiled=True)


def choose(rows, cols, first, scale, offset):
    row = lax.broadcasted_iota(jnp.int32, (rows, cols), 0) + first
    col = lax.broadcasted_iota(jnp.int32, (rows, cols), 1) * scale + offset
    return (row == col).astype(F32).astype(BF16)


def make_kernel(cells, scens, scen_rows, cell_rows, bwidth, twidth, groups, classes, samples, feats,
                own_rows, pairs):
    pad_rows = -(-own_rows // 16) * 16
    chunk = scen_rows // cells
    in_rows = 2 * (samples + groups)
    branch_rows = in_rows + bwidth
    trunk_lead = feats + classes
    all_scen = scens * scen_rows
    inv_root = 1.0 / math.sqrt(WIDE)
    inv_pairs = 1.0 / math.sqrt(pairs)
    trunk_dests = [
        d for d in range(cells) if ((d + 1) * scens) * own_rows > branch_rows
    ]
    tile = 128

    def kernel(hydro, group, feat, klass, b_in, g_tab, b_out, t_in, c_tab, t_out, targets, out,
               x_all, w_b, w_t, x_t, dgelu, hid, coeff, hid_t, basis, resid, part_f, part_b,
               part_in, dc, dbasis, dpre_t, pick_in0, pick_in1, pick_hid, t_own, t_send, t_recv,
               dpre_b, total,
               x_ss, x_rs, r_ss, r_rs, p_ss, p_rs, z_ss, z_rs, d_ss, d_rs, t_ss, t_rs):
        c = lax.axis_index("cell")
        s = lax.axis_index("scen")
        first = (c * scens + s) * own_rows

        def scen_at(k):
            return lax.rem(s + k, scens)

        def cell_at(k):
            return lax.rem(c + k, cells)

        def to_scen(src, dst, ss, rs, k):
            return pltpu.make_async_remote_copy(
                src_ref=src, dst_ref=dst, send_sem=ss.at[k - 1], recv_sem=rs.at[k - 1],
                device_id={"scen": scen_at(k)}, device_id_type=MESH)

        def to_cell(src, dst, ss, rs, k):
            return pltpu.make_async_remote_copy(
                src_ref=src, dst_ref=dst, send_sem=ss.at[k - 1], recv_sem=rs.at[k - 1],
                device_id={"cell": cell_at(k)}, device_id_type=MESH)

        barrier = pltpu.get_barrier_semaphore()
        for k in range(1, scens):
            pl.semaphore_signal(barrier, inc=1, device_id={"scen": scen_at(k)}, device_id_type=MESH)
        for k in range(1, cells):
            pl.semaphore_signal(barrier, inc=1, device_id={"cell": cell_at(k)}, device_id_type=MESH)

        hot = (lax.broadcasted_iota(jnp.int32, (128, scen_rows), 0) == group[...]).astype(F32)
        x_all[s, :, 0:samples] = hydro[...]
        x_all[s, :, samples:samples + 128] = hot.T.astype(BF16)
        pl.semaphore_wait(barrier, scens + cells - 2)
        x_copies = [to_scen(x_all.at[s], x_all.at[s], x_ss, x_rs, k) for k in range(1, scens)]
        for copy in x_copies:
            copy.start()

        w_b[0:samples, :] = b_in[...]
        w_b[samples:samples + groups, :] = g_tab[...]
        w_b[samples + groups:, :] = jnp.zeros((128 - groups, bwidth), BF16)
        w_t[0:feats, :] = t_in[...]
        w_t[feats:feats + classes, :] = c_tab[...]
        w_t[feats + classes:, :] = jnp.zeros((128 - classes, twidth), BF16)

        def branch(p):
            pre = contract(x_all[p], w_b[...], 1, 0)
            inner = math.sqrt(2.0 / math.pi)
            bent = jnp.tanh(inner * (pre + 0.044715 * (pre * pre * pre)))
            cdf = 0.5 * (1.0 + bent)
            hid[p] = (pre * cdf).astype(BF16)
            dgelu[p] = cdf + (0.5 * inner) * pre * (1.0 - bent * bent) * (
                1.0 + (3.0 * 0.044715) * (pre * pre))
            coeff[p] = contract(hid[p], b_out[...], 1, 0).astype(BF16)

        branch(s)

        @pl.loop(0, cell_rows // tile)
        def _(b):
            rows = pl.ds(pl.multiple_of(b * tile, tile), tile)
            x_t[rows, 0:feats] = feat[rows, :]
            lane = lax.broadcasted_iota(jnp.int32, (tile, 128), 1)
            x_t[rows, feats:feats + 128] = (lane == klass[b]).astype(F32).astype(BF16)
            pre = contract(x_t[rows, :], w_t[...], 1, 0)
            hid_t[rows, :] = jnp.tanh(pre).astype(BF16)
            basis[rows, :] = contract(hid_t[rows, :], t_out[...], 1, 0).astype(BF16)

        predicted = contract(coeff[s], basis[...], 1, 1) * inv_root
        resid[s] = ((predicted - targets[...]) * inv_pairs).astype(BF16)
        r_copies = [to_scen(resid.at[s], resid.at[s], r_ss, r_rs, k) for k in range(1, scens)]
        for copy in r_copies:
            copy.start()
        partial = contract(resid[s], basis[...], 1, 0)
        for d in range(cells):
            part_f[d] = partial[d * chunk:(d + 1) * chunk]
            part_b[d] = partial[d * chunk:(d + 1) * chunk].astype(BF16)
        p_copies = [to_cell(part_b.at[cell_at(k)], part_in.at[k - 1], p_ss, p_rs, k)
                    for k in range(1, cells)]
        for copy in p_copies:
            copy.start()

        for copy in x_copies:
            copy.wait()
        @pl.loop(1, scens)
        def _(k):
            branch(lax.rem(s + k, scens))

        for copy in p_copies:
            copy.wait()
        summed = part_f[c]
        for k in range(cells - 1):
            summed = summed + part_in[k].astype(F32)
        dc[s, c] = summed.astype(BF16)
        z_copies = [to_cell(dc.at[s, c], dc.at[s, c], z_ss, z_rs, k) for k in range(1, cells)]
        for copy in z_copies:
            copy.start()

        for copy in r_copies:
            copy.wait()
        @pl.loop(0, cell_rows // tile)
        def _(b):
            cols = pl.ds(pl.multiple_of(b * tile, tile), tile)
            sums = jnp.zeros((tile, WIDE), F32)
            for p in range(scens):
                sums = sums + contract(resid[p, :, cols], coeff[p], 0, 0)
            dbasis[cols, :] = sums.astype(BF16)

        def trunk_need(d, me):
            return (d * scens + me + 1) * own_rows > branch_rows

        def lead_need(d, me):
            return ((d * scens + me + 1) * own_rows > branch_rows) & (
                (d * scens + me) * own_rows < branch_rows + trunk_lead)

        lead_any = lead_need(trunk_dests[0], s)
        for d in trunk_dests[1:]:
            lead_any = lead_any | lead_need(d, s)

        @pl.when(lead_any)
        def _():
            @pl.loop(0, cell_rows // tile)
            def _(b):
                rows = pl.ds(pl.multiple_of(b * tile, tile), tile)
                h = contract(x_t[rows, :], w_t[...], 1, 0)
                h = jnp.tanh(h)
                d_hid = contract(dbasis[rows, :], t_out[...], 1, 1)
                dpre_t[rows, :] = ((1.0 - h * h) * d_hid).astype(BF16)

        def t_copy(at, d):
            slot = lax.rem(c + cells - d, cells) - 1
            return pltpu.make_async_remote_copy(
                src_ref=t_send.at[at], dst_ref=t_recv.at[slot], send_sem=t_ss.at[at],
                recv_sem=t_rs.at[slot], device_id={"cell": d}, device_id_type=MESH)

        for at, d in reversed(list(enumerate(trunk_dests))):
            @pl.when(trunk_need(d, s))
            def _():
                base = (d * scens + s) * own_rows
                pick = contract(
                    choose(pad_rows, twidth, base, 1, branch_rows + trunk_lead), hid_t[...], 1, 1)
                total[...] = contract(pick.astype(BF16), dbasis[...], 1, 0)

                @pl.when(lead_need(d, s))
                def _():
                    pick = contract(
                        choose(pad_rows, feats + 128, base, 1, branch_rows)
                        * (lax.broadcasted_iota(jnp.int32, (pad_rows, feats + 128), 1)
                           < trunk_lead).astype(F32).astype(BF16),
                        x_t[...], 1, 1)
                    total[...] += contract(pick.astype(BF16), dpre_t[...], 1, 0)

                @pl.when(c == d)
                def _():
                    t_own[...] = total[...]

                @pl.when(c != d)
                def _():
                    t_send[at] = total[...].astype(BF16)
                    t_copy(at, d).start()

        for copy in z_copies:
            copy.wait()
        d_copies = [to_scen(dc.at[s], dc.at[s], d_ss, d_rs, k) for k in range(1, scens)]
        for copy in d_copies:
            copy.start()

        has_in = first < in_rows
        has_hid = (first + own_rows > in_rows) & (first < branch_rows)
        has_trunk = first + own_rows > branch_rows
        x_whole = x_all.reshape(all_scen, samples + 128)
        hid_whole = hid.reshape(all_scen, bwidth)

        @pl.when(has_in)
        def _():
            keep = (lax.broadcasted_iota(jnp.int32, (pad_rows, samples + 128), 1)
                    < samples + groups).astype(F32).astype(BF16)
            pick_in0[...] = contract(choose(pad_rows, samples + 128, first, 2, 0) * keep,
                                     x_whole[...], 1, 1).astype(BF16)
            pick_in1[...] = contract(choose(pad_rows, samples + 128, first, 2, 1) * keep,
                                     x_whole[...], 1, 1).astype(BF16)

        @pl.when(has_hid)
        def _():
            pick_hid[...] = contract(choose(pad_rows, bwidth, first, 1, in_rows),
                                     hid_whole[...], 1, 1).astype(BF16)

        total[...] = jnp.zeros_like(total)
        for copy in d_copies:
            copy.wait()
        dc_whole = dc.reshape(all_scen, WIDE)

        @pl.when(has_hid)
        def _():
            total[...] += contract(pick_hid[...], dc_whole[...], 1, 0)

        @pl.when(has_in)
        def _():
            dc_rows = dc.reshape(scens, scen_rows, WIDE)
            @pl.loop(0, scens)
            def _(p):
                d_hid = contract(dc_rows[p], b_out[...], 1, 1)
                rows = pl.ds(pl.multiple_of(p * scen_rows, scen_rows), scen_rows)
                dpre_b[rows, :] = (d_hid * dgelu[p]).astype(BF16)
            total[...] += contract(pick_in0[...], dpre_b[:, :WIDE], 1, 0)
            total[...] += contract(pick_in1[...], dpre_b[:, WIDE:], 1, 0)

        @pl.when(has_trunk)
        def _():
            total[...] += t_own[...]
            for k in range(cells - 1):
                pltpu.make_async_remote_copy(
                    src_ref=t_send.at[0], dst_ref=t_recv.at[k], send_sem=t_ss.at[0],
                    recv_sem=t_rs.at[k], device_id={"cell": cell_at(1)},
                    device_id_type=MESH).wait_recv()
                total[...] += t_recv[k].astype(F32)

        for j in range(WIDE // 128):
            out[pl.ds(j, own_rows, WIDE // 128), :] = total[0:own_rows, j * 128:(j + 1) * 128]

        for at, d in enumerate(trunk_dests):
            @pl.when(trunk_need(d, s) & (c != d))
            def _():
                t_copy(at, d).wait_send()

    dma = pltpu.SemaphoreType.DMA
    scratch = [
        pltpu.VMEM((scens, scen_rows, samples + 128), BF16),
        pltpu.VMEM((samples + 128, bwidth), BF16),
        pltpu.VMEM((feats + 128, twidth), BF16),
        pltpu.VMEM((cell_rows, feats + 128), BF16),
        pltpu.VMEM((scens, scen_rows, bwidth), F32),
        pltpu.VMEM((scens, scen_rows, bwidth), BF16),
        pltpu.VMEM((scens, scen_rows, WIDE), BF16),
        pltpu.VMEM((cell_rows, twidth), BF16),
        pltpu.VMEM((cell_rows, WIDE), BF16),
        pltpu.VMEM((scens, scen_rows, cell_rows), BF16),
        pltpu.VMEM((cells, chunk, WIDE), F32),
        pltpu.VMEM((cells, chunk, WIDE), BF16),
        pltpu.VMEM((cells - 1, chunk, WIDE), BF16),
        pltpu.VMEM((scens, cells, chunk, WIDE), BF16),
        pltpu.VMEM((cell_rows, WIDE), BF16),
        pltpu.VMEM((cell_rows, twidth), BF16),
        pltpu.VMEM((pad_rows, all_scen), BF16),
        pltpu.VMEM((pad_rows, all_scen), BF16),
        pltpu.VMEM((pad_rows, all_scen), BF16),
        pltpu.VMEM((pad_rows, WIDE), F32),
        pltpu.VMEM((len(trunk_dests), pad_rows, WIDE), BF16),
        pltpu.VMEM((cells - 1, pad_rows, WIDE), BF16),
        pltpu.VMEM((all_scen, bwidth), BF16),
        pltpu.VMEM((pad_rows, WIDE), F32),
        dma((scens - 1,)), dma((scens - 1,)),
        dma((scens - 1,)), dma((scens - 1,)),
        dma((cells - 1,)), dma((cells - 1,)),
        dma((cells - 1,)), dma((cells - 1,)),
        dma((scens - 1,)), dma((scens - 1,)),
        dma((len(trunk_dests),)), dma((cells - 1,)),
    ]
    return kernel, scratch


def shards(hydrograph, scen_group, cell_feat, cell_class, branch_in, group_table, branch_out,
           trunk_in, class_table, trunk_out, targets):
    cells = lax.axis_size("cell")
    scens = lax.axis_size("scen")
    scen_rows, samples = hydrograph.shape
    cell_rows, feats = cell_feat.shape
    bwidth, width = branch_out.shape
    twidth = trunk_in.shape[1]
    groups, classes = group_table.shape[0], class_table.shape[0]
    size = (samples + groups + width) * bwidth + (feats + classes + width) * twidth
    block = size // (cells * scens)
    fits = (
        cells > 1 and scens > 1 and width == WIDE and twidth == WIDE and bwidth == 2 * WIDE
        and block % WIDE == 0 and block * cells * scens == size
        and scen_rows == 128 and scen_rows % (16 * cells) == 0 and cell_rows % 128 == 0
        and samples == 128 and feats == 128 and groups <= 128 and classes <= 128
        and groups % 16 == 0 and classes % 16 == 0 and scens * scen_rows <= 1024
        and cell_rows <= 512
    )
    if not fits:
        return plain_shards(hydrograph, scen_group, cell_feat, cell_class, branch_in, group_table,
                            branch_out, trunk_in, class_table, trunk_out, targets)
    pairs = float(scen_rows * scens) * float(cell_rows * cells)
    kernel, scratch = make_kernel(cells, scens, scen_rows, cell_rows, bwidth, twidth, groups,
                                  classes, samples, feats, block // WIDE, pairs)
    vmem = pl.BlockSpec(memory_space=pltpu.VMEM)
    smem = pl.BlockSpec(memory_space=pltpu.SMEM)
    out = pl.pallas_call(
        kernel,
        out_shape=jax.ShapeDtypeStruct((block // 128, 128), F32),
        in_specs=[vmem, vmem, vmem, smem] + [vmem] * 7,
        out_specs=vmem,
        scratch_shapes=scratch,
        compiler_params=pltpu.CompilerParams(
            collective_id=0, has_side_effects=True, vmem_limit_bytes=40 * 1024 * 1024),
    )(hydrograph, scen_group.reshape(1, scen_rows), cell_feat, cell_class, branch_in, group_table,
      branch_out, trunk_in, class_table, trunk_out, targets)
    return out.reshape(block)


def solution(mesh):
    in_specs = (
        P(("rep", "scen"), None),
        P(("rep", "scen")),
        P(("rep", "cell"), None),
        P(("rep", "cell")),
        P(),
        P(),
        P(),
        P(),
        P(),
        P(),
        P(("rep", "scen"), "cell"),
    )
    out_specs = P(("rep", "cell", "scen"))
    return jax.shard_map(shards, mesh=mesh, in_specs=in_specs, out_specs=out_specs, check_vma=False)
```

time: 178 us -> 38.8 us (0.22)
  waiting for transfers between devices: 110 us -> 0 us
  Pallas kernels: 0 us -> 28.7 us
  blocking collectives: 20.6 us -> 0 us
  between operations: 14.3 us -> 0.02 us
  matrix products: 12.9 us -> 0 us
  other arithmetic: 5.56 us -> 0 us
  local copies, waits for them, and re-layouts: 12.1 us -> 9.59 us
    unnamed x3 -> x0, waiting for transfers between devices: 110 us -> none
    pallas_call x0 -> x1, Pallas kernels: none -> 28.7 us  [shards(): pl.pallas_call(kernel, out_shape=jax.ShapeDtypeStruct((block // 128, 128)...]
    psum x1 -> x0, blocking collectives: 20.6 us -> none  [shards(): lax.psum(jnp.dot(resid, basis_local, preferred_element_type=jnp.float32),...]
    dot_general x17 -> x0, matrix products: 12.9 us -> none  [the longest x10 8.98 us: contract(): lax.dot_general(left, right, (((left_dim,), (right_dim,)), ((), ())), pre...]
    mul x2 -> x0, other arithmetic: 3.39 us -> none  [the longest x1 3.29 us: shards(): branch_flat * (lax.axis_index('cell') == 0).astype(jnp.float32)]
    concatenate x1 -> x0, other arithmetic: 2.17 us -> none  [shards(): flat_grad = jnp.concatenate([branch_flat, trunk_flat])]
    unnamed x34 -> x23, local copies, waits for them, and re-layouts: 10.2 us -> 9.59 us
  transfers between devices with their start and end apart: 2 -> 0, of which waited for: 1 -> 0; matrix products, arithmetic and copies ran while one was open for 8% -> 0% of each run, Pallas kernels for 0% -> 0%
where the time goes in v1:
time: 38.8 us; the launch traced here: 38.3 us
  Pallas kernels  28.7 us (74%)
  local copies, waits for them, and re-layouts  9.59 us (25%)
    pallas_call x1, Pallas kernels, shards(): pl.pallas_call(kernel, out_shape=jax.ShapeDtypeStruct((block // 128, 128)...  28.7 us
    unnamed x23, local copies, waits for them, and re-layouts  9.59 us

profile of v1, /device:TPU:1, one launch (start us, length us, event | category | flops | bytes accessed | tf_op | source)
XLA Modules:
  0.0 38.3 jit_solution(11323646141564534459)
XLA Ops:
  0.0 0.0 copy-start.10
  0.0 0.0 copy-start.9
  0.0 0.7 %copy-done.10 = s32[4]{0:T(128)S(1)} copy-done((s32[4]{0:T(128)S(1)}, s32[4]{0:T(128)}, u32[]{:S(2)}) %copy-start.10) | copy-done | bytes 40
  0.7 0.0 copy-done.9
  0.7 0.0 copy-start
  0.7 1.2 %copy-done = bf16[1024,512]{1,0:T(8,128)(2,1)S(1)} copy-done((bf16[1024,512]{1,0:T(8,128)(2,1)S(1)}, bf16[1024,512]{1,0:T(8,128)(2,1)}, u32[]{:S(2)}) %copy-start) | copy-done | bytes 1048600
  1.9 0.0 copy-start.1
  1.9 1.0 %copy-done.1 = bf16[512,512]{1,0:T(8,128)(2,1)S(1)} copy-done((bf16[512,512]{1,0:T(8,128)(2,1)S(1)}, bf16[512,512]{1,0:T(8,128)(2,1)}, u32[]{:S(2)}) %copy-start.1) | copy-done | bytes 524312
  2.9 0.0 copy-start.2
  2.9 0.9 %copy-done.2 = bf16[128,1024]{1,0:T(8,128)(2,1)S(1)} copy-done((bf16[128,1024]{1,0:T(8,128)(2,1)S(1)}, bf16[128,1024]{1,0:T(8,128)(2,1)}, u32[]{:S(2)}) %copy-start.2) | copy-done | bytes 262168
  3.9 0.0 copy-start.3
  3.9 0.9 %copy-done.3 = f32[128,512]{1,0:T(8,128)S(1)} copy-done((f32[128,512]{1,0:T(8,128)S(1)}, f32[128,512]{1,0:T(8,128)}, u32[]{:S(2)}) %copy-start.3) | copy-done | bytes 262168
  4.8 0.0 copy-start.4
  4.8 0.9 %copy-done.4 = bf16[512,128]{1,0:T(8,128)(2,1)S(1)} copy-done((bf16[512,128]{1,0:T(8,128)(2,1)S(1)}, bf16[512,128]{1,0:T(8,128)(2,1)}, u32[]{:S(2)}) %copy-start.4) | copy-done | bytes 131096
  5.7 0.0 copy-start.5
  5.7 0.9 %copy-done.5 = bf16[128,512]{1,0:T(8,128)(2,1)S(1)} copy-done((bf16[128,512]{1,0:T(8,128)(2,1)S(1)}, bf16[128,512]{1,0:T(8,128)(2,1)}, u32[]{:S(2)}) %copy-start.5) | copy-done | bytes 131096
  6.7 0.0 copy-start.6
  6.7 0.8 %copy-done.6 = bf16[128,128]{1,0:T(8,128)(2,1)S(1)} copy-done((bf16[128,128]{1,0:T(8,128)(2,1)S(1)}, bf16[128,128]{1,0:T(8,128)(2,1)}, u32[]{:S(2)}) %copy-start.6) | copy-done | bytes 32792
  7.4 0.0 copy-start.7
  7.4 0.8 %copy-done.7 = bf16[16,1024]{1,0:T(8,128)(2,1)S(1)} copy-done((bf16[16,1024]{1,0:T(8,128)(2,1)S(1)}, bf16[16,1024]{1,0:T(8,128)(2,1)}, u32[]{:S(2)}) %copy-start.7) | copy-done | bytes 32792
  8.2 0.0 copy-start.8
  8.2 0.7 %copy-done.8 = bf16[16,512]{1,0:T(8,128)(2,1)S(1)} copy-done((bf16[16,512]{1,0:T(8,128)(2,1)S(1)}, bf16[16,512]{1,0:T(8,128)(2,1)}, u32[]{:S(2)}) %copy-start.8) | copy-done | bytes 16408
  8.9 28.7 %shard_map.109 = f32[492,128]{1,0:T(8,128)S(1)} custom-call(bf16[128,128]{1,0:T(8,128)(2,1)S(1)} %copy-done.6, s32[1,128]{1,0:T(1,128)S(1)} %bitcast.3, bf16[512,128]{1,0:T(8,128)(2,1)S(1)} %copy-done.4, s32[4]{0:T(128)S(1)} %copy-done.10, bf16[128,1024]{1,0:T(8,128)(2,1)S(1)} %copy-done.2, bf16[16,1024]{1,0:T(8,128)(2,1)S(1)} %copy-done.7, ...), custom_call_target="tpu_custom_call" | custom-call | tf_op jit(solution)/shard_map/pallas_call | solution.py:388
  37.6 0.7 %copy.13 = f32[62976]{0:T(1024)} copy(f32[62976]{0:T(1024)S(1)} %bitcast.2) | data formatting | bytes 503808
Async XLA Ops:
  0.0 0.7 %copy-start.10 = (s32[4]{0:T(128)S(1)}, s32[4]{0:T(128)}, u32[]{:S(2)}) copy-start(s32[4]{0:T(128)} %klass.1) | copy-start | bytes 52
  0.0 0.7 %copy-start.9 = (s32[128]{0:T(128)S(1)}, s32[128]{0:T(128)}, u32[]{:S(2)}) copy-start(s32[128]{0:T(128)} %param.12) | copy-start | bytes 1540
  0.7 1.2 %copy-start = (bf16[1024,512]{1,0:T(8,128)(2,1)S(1)}, bf16[1024,512]{1,0:T(8,128)(2,1)}, u32[]{:S(2)}) copy-start(bf16[1024,512]{1,0:T(8,128)(2,1)} %b_out.1) | copy-start | bytes 3145732
  1.9 1.0 %copy-start.1 = (bf16[512,512]{1,0:T(8,128)(2,1)S(1)}, bf16[512,512]{1,0:T(8,128)(2,1)}, u32[]{:S(2)}) copy-start(bf16[512,512]{1,0:T(8,128)(2,1)} %t_out.1) | copy-start | bytes 1572868
  2.9 0.9 %copy-start.2 = (bf16[128,1024]{1,0:T(8,128)(2,1)S(1)}, bf16[128,1024]{1,0:T(8,128)(2,1)}, u32[]{:S(2)}) copy-start(bf16[128,1024]{1,0:T(8,128)(2,1)} %b_in.1) | copy-start | bytes 786436
  3.9 0.9 %copy-start.3 = (f32[128,512]{1,0:T(8,128)S(1)}, f32[128,512]{1,0:T(8,128)}, u32[]{:S(2)}) copy-start(f32[128,512]{1,0:T(8,128)} %targets.1) | copy-start | bytes 786436
  4.8 0.9 %copy-start.4 = (bf16[512,128]{1,0:T(8,128)(2,1)S(1)}, bf16[512,128]{1,0:T(8,128)(2,1)}, u32[]{:S(2)}) copy-start(bf16[512,128]{1,0:T(8,128)(2,1)} %feat.1) | copy-start | bytes 393220
  5.7 0.9 %copy-start.5 = (bf16[128,512]{1,0:T(8,128)(2,1)S(1)}, bf16[128,512]{1,0:T(8,128)(2,1)}, u32[]{:S(2)}) copy-start(bf16[128,512]{1,0:T(8,128)(2,1)} %t_in.1) | copy-start | bytes 393220
  6.7 0.8 %copy-start.6 = (bf16[128,128]{1,0:T(8,128)(2,1)S(1)}, bf16[128,128]{1,0:T(8,128)(2,1)}, u32[]{:S(2)}) copy-start(bf16[128,128]{1,0:T(8,128)(2,1)} %hydro.1) | copy-start | bytes 98308
  7.4 0.8 %copy-start.7 = (bf16[16,1024]{1,0:T(8,128)(2,1)S(1)}, bf16[16,1024]{1,0:T(8,128)(2,1)}, u32[]{:S(2)}) copy-start(bf16[16,1024]{1,0:T(8,128)(2,1)} %g_tab.1) | copy-start | bytes 98308
  8.2 0.7 %copy-start.8 = (bf16[16,512]{1,0:T(8,128)(2,1)S(1)}, bf16[16,512]{1,0:T(8,128)(2,1)}, u32[]{:S(2)}) copy-start(bf16[16,512]{1,0:T(8,128)(2,1)} %c_tab.1) | copy-start | bytes 49156

commit v2 on v1

--- a/solution.py
+++ b/solution.py
@@ -97,8 +97,9 @@
     ]
     tile = 128
 
-    def kernel(hydro, group, feat, klass, b_in, g_tab, b_out, t_in, c_tab, t_out, targets, out,
-               x_all, w_b, w_t, x_t, dgelu, hid, coeff, hid_t, basis, resid, part_f, part_b,
+    def kernel(hydro, group_h, feat, klass_h, b_in, g_tab, b_out_h, t_in, c_tab, t_out_h,
+               targets_h, out,
+               group, klass, b_out, t_out, targets, in_sem, x_all, w_b, w_t, x_t, dgelu, hid, coeff, hid_t, basis, resid, part_f, part_b,
                part_in, dc, dbasis, dpre_t, pick_in0, pick_in1, pick_hid, t_own, t_send, t_recv,
                dpre_b, total,
                x_ss, x_rs, r_ss, r_rs, p_ss, p_rs, z_ss, z_rs, d_ss, d_rs, t_ss, t_rs):
@@ -122,25 +123,40 @@
                 src_ref=src, dst_ref=dst, send_sem=ss.at[k - 1], recv_sem=rs.at[k - 1],
                 device_id={"cell": cell_at(k)}, device_id_type=MESH)
 
+        loads = [
+            pltpu.make_async_copy(src, dst, in_sem.at[at])
+            for at, (src, dst) in enumerate([
+                (group_h, group),
+                (hydro, x_all.at[s, :, 0:samples]),
+                (b_in, w_b.at[0:samples]),
+                (g_tab, w_b.at[samples:samples + groups]),
+                (b_out_h, b_out),
+                (feat, x_t.at[:, 0:feats]),
+                (klass_h, klass),
+                (t_in, w_t.at[0:feats]),
+                (c_tab, w_t.at[feats:feats + classes]),
+                (t_out_h, t_out),
+                (targets_h, targets),
+            ])
+        ]
+        for load in loads:
+            load.start()
         barrier = pltpu.get_barrier_semaphore()
         for k in range(1, scens):
             pl.semaphore_signal(barrier, inc=1, device_id={"scen": scen_at(k)}, device_id_type=MESH)
         for k in range(1, cells):
             pl.semaphore_signal(barrier, inc=1, device_id={"cell": cell_at(k)}, device_id_type=MESH)
 
+        loads[0].wait()
+        loads[1].wait()
         hot = (lax.broadcasted_iota(jnp.int32, (128, scen_rows), 0) == group[...]).astype(F32)
-        x_all[s, :, 0:samples] = hydro[...]
         x_all[s, :, samples:samples + 128] = hot.T.astype(BF16)
         pl.semaphore_wait(barrier, scens + cells - 2)
         x_copies = [to_scen(x_all.at[s], x_all.at[s], x_ss, x_rs, k) for k in range(1, scens)]
         for copy in x_copies:
             copy.start()
 
-        w_b[0:samples, :] = b_in[...]
-        w_b[samples:samples + groups, :] = g_tab[...]
         w_b[samples + groups:, :] = jnp.zeros((128 - groups, bwidth), BF16)
-        w_t[0:feats, :] = t_in[...]
-        w_t[feats:feats + classes, :] = c_tab[...]
         w_t[feats + classes:, :] = jnp.zeros((128 - classes, twidth), BF16)
 
         def branch(p):
@@ -153,18 +169,22 @@
                 1.0 + (3.0 * 0.044715) * (pre * pre))
             coeff[p] = contract(hid[p], b_out[...], 1, 0).astype(BF16)
 
+        for load in loads[2:5]:
+            load.wait()
         branch(s)
+        for load in loads[5:10]:
+            load.wait()
 
         @pl.loop(0, cell_rows // tile)
         def _(b):
             rows = pl.ds(pl.multiple_of(b * tile, tile), tile)
-            x_t[rows, 0:feats] = feat[rows, :]
             lane = lax.broadcasted_iota(jnp.int32, (tile, 128), 1)
             x_t[rows, feats:feats + 128] = (lane == klass[b]).astype(F32).astype(BF16)
             pre = contract(x_t[rows, :], w_t[...], 1, 0)
             hid_t[rows, :] = jnp.tanh(pre).astype(BF16)
             basis[rows, :] = contract(hid_t[rows, :], t_out[...], 1, 0).astype(BF16)
 
+        loads[10].wait()
         predicted = contract(coeff[s], basis[...], 1, 1) * inv_root
         resid[s] = ((predicted - targets[...]) * inv_pairs).astype(BF16)
         r_copies = [to_scen(resid.at[s], resid.at[s], r_ss, r_rs, k) for k in range(1, scens)]
@@ -324,6 +344,12 @@
 
     dma = pltpu.SemaphoreType.DMA
     scratch = [
+        pltpu.VMEM((1, scen_rows), jnp.int32),
+        pltpu.SMEM((cell_rows // 128,), jnp.int32),
+        pltpu.VMEM((bwidth, WIDE), BF16),
+        pltpu.VMEM((twidth, WIDE), BF16),
+        pltpu.VMEM((scen_rows, cell_rows), F32),
+        dma((11,)),
         pltpu.VMEM((scens, scen_rows, samples + 128), BF16),
         pltpu.VMEM((samples + 128, bwidth), BF16),
         pltpu.VMEM((feats + 128, twidth), BF16),
@@ -384,15 +410,15 @@
     kernel, scratch = make_kernel(cells, scens, scen_rows, cell_rows, bwidth, twidth, groups,
                                   classes, samples, feats, block // WIDE, pairs)
     vmem = pl.BlockSpec(memory_space=pltpu.VMEM)
-    smem = pl.BlockSpec(memory_space=pltpu.SMEM)
+    hbm = pl.BlockSpec(memory_space=pltpu.HBM)
     out = pl.pallas_call(
         kernel,
         out_shape=jax.ShapeDtypeStruct((block // 128, 128), F32),
-        in_specs=[vmem, vmem, vmem, smem] + [vmem] * 7,
+        in_specs=[hbm] * 11,
         out_specs=vmem,
         scratch_shapes=scratch,
         compiler_params=pltpu.CompilerParams(
-            collective_id=0, has_side_effects=True, vmem_limit_bytes=40 * 1024 * 1024),
+            collective_id=0, has_side_effects=True, vmem_limit_bytes=64 * 1024 * 1024),
     )(hydrograph, scen_group.reshape(1, scen_rows), cell_feat, cell_class, branch_in, group_table,
       branch_out, trunk_in, class_table, trunk_out, targets)
     return out.reshape(block)

time: 38.8 us -> 30.7 us (0.79)
  local copies, waits for them, and re-layouts: 9.59 us -> 1.66 us
    unnamed x23 -> x1, local copies, waits for them, and re-layouts: 9.59 us -> 1.66 us
where the time goes in v2:
time: 30.7 us; the launch traced here: 30.6 us
  Pallas kernels  28.9 us (94%)
  local copies, waits for them, and re-layouts  1.66 us (5%)
    pallas_call x1, Pallas kernels, shards(): pl.pallas_call(kernel, out_shape=jax.ShapeDtypeStruct((block // 128, 128)...  28.9 us
    unnamed x1, local copies, waits for them, and re-layouts  1.66 us

profile of v2, /device:TPU:1, one launch (start us, length us, event | category | flops | bytes accessed | tf_op | source)
XLA Modules:
  0.0 30.6 jit_solution(7350280149941670410)
XLA Ops:
  0.0 28.9 %shard_map.109 = f32[492,128]{1,0:T(8,128)} custom-call(bf16[128,128]{1,0:T(8,128)(2,1)} %hydro.1, s32[1,128]{1,0:T(1,128)} %bitcast.3, bf16[512,128]{1,0:T(8,128)(2,1)} %feat.1, s32[4]{0:T(128)} %klass_h.1, bf16[128,1024]{1,0:T(8,128)(2,1)} %b_in.1, bf16[16,1024]{1,0:T(8,128)(2,1)} %g_tab.1, bf16[1024,512]{1,0:T(8,128)(2,1)} %b_out_h.1, ...), custom_call_target="tpu_custom_call" | custom-call | tf_op jit(solution)/shard_map/pallas_call | solution.py:414
  28.9 1.7 %copy.13 = f32[62976]{0:T(1024)} copy(f32[62976]{0:T(1024)} %bitcast.2) | data formatting | bytes 503808

commit v3 on v2

--- a/solution.py
+++ b/solution.py
@@ -96,13 +96,14 @@
         d for d in range(cells) if ((d + 1) * scens) * own_rows > branch_rows
     ]
     tile = 128
+    branch_cells = -(-branch_rows // (scens * own_rows))
 
     def kernel(hydro, group_h, feat, klass_h, b_in, g_tab, b_out_h, t_in, c_tab, t_out_h,
                targets_h, out,
                group, klass, b_out, t_out, targets, in_sem, x_all, w_b, w_t, x_t, dgelu, hid, coeff, hid_t, basis, resid, part_f, part_b,
-               part_in, dc, dbasis, dpre_t, pick_in0, pick_in1, pick_hid, t_own, t_send, t_recv,
+               part_in, dc, dbasis, dpre_t, pick_in0, pick_in1, pick_hid, t_own, t_send, t_recv, t_mid, t_relay,
                dpre_b, total,
-               x_ss, x_rs, r_ss, r_rs, p_ss, p_rs, z_ss, z_rs, d_ss, d_rs, t_ss, t_rs):
+               x_ss, x_rs, r_ss, r_rs, p_ss, p_rs, z_ss, z_rs, f_ss, f_rs, n_ss, n_rs, g_ss, g_rs, t_ss, t_rs, m_rs):
         c = lax.axis_index("cell")
         s = lax.axis_index("scen")
         first = (c * scens + s) * own_rows
@@ -112,6 +113,14 @@
 
         def cell_at(k):
             return lax.rem(c + k, cells)
+
+        sibling = s + 1 - 2 * lax.rem(s, 2)
+        far = lax.rem(s + scens // 2, scens)
+
+        def to_peer(ref, ss, rs, at, peer):
+            return pltpu.make_async_remote_copy(
+                src_ref=ref, dst_ref=ref, send_sem=ss.at[at], recv_sem=rs.at[at],
+                device_id={"scen": peer}, device_id_type=MESH)
 
         def to_scen(src, dst, ss, rs, k):
             return pltpu.make_async_remote_copy(
@@ -187,9 +196,10 @@
         loads[10].wait()
         predicted = contract(coeff[s], basis[...], 1, 1) * inv_root
         resid[s] = ((predicted - targets[...]) * inv_pairs).astype(BF16)
-        r_copies = [to_scen(resid.at[s], resid.at[s], r_ss, r_rs, k) for k in range(1, scens)]
-        for copy in r_copies:
-            copy.start()
+        r_far = to_peer(resid.at[s], r_ss, r_rs, 0, far)
+        r_far.start()
+        r_near = to_peer(resid.at[s], r_ss, r_rs, 1, sibling)
+        r_near.start()
         partial = contract(resid[s], basis[...], 1, 0)
         for d in range(cells):
             part_f[d] = partial[d * chunk:(d + 1) * chunk]
@@ -205,6 +215,9 @@
         def _(k):
             branch(lax.rem(s + k, scens))
 
+        r_far.wait()
+        r_pass = to_peer(resid.at[far], r_ss, r_rs, 2, sibling)
+        r_pass.start()
         for copy in p_copies:
             copy.wait()
         summed = part_f[c]
@@ -212,11 +225,27 @@
             summed = summed + part_in[k].astype(F32)
         dc[s, c] = summed.astype(BF16)
         z_copies = [to_cell(dc.at[s, c], dc.at[s, c], z_ss, z_rs, k) for k in range(1, cells)]
-        for copy in z_copies:
-            copy.start()
-
-        for copy in r_copies:
-            copy.wait()
+        takes_dc = c < branch_cells
+
+        def share(j):
+            chunk_at = dc.at[s, lax.rem(c + cells - j, cells)]
+            return [to_peer(chunk_at, f_ss, f_rs, j, far), to_peer(chunk_at, n_ss, n_rs, j, sibling)]
+
+        def pass_on(j):
+            return to_peer(dc.at[far, lax.rem(c + cells - j, cells)], g_ss, g_rs, j, sibling)
+
+        for k, copy in enumerate(z_copies):
+            @pl.when(cell_at(k + 1) < branch_cells)
+            def _():
+                copy.start()
+
+        @pl.when(takes_dc)
+        def _():
+            for copy in share(0):
+                copy.start()
+
+        r_near.wait()
+        r_pass.wait()
         @pl.loop(0, cell_rows // tile)
         def _(b):
             cols = pl.ds(pl.multiple_of(b * tile, tile), tile)
@@ -246,11 +275,15 @@
                 d_hid = contract(dbasis[rows, :], t_out[...], 1, 1)
                 dpre_t[rows, :] = ((1.0 - h * h) * d_hid).astype(BF16)
 
-        def t_copy(at, d):
-            slot = lax.rem(c + cells - d, cells) - 1
+        def t_copy(at, d, relay):
             return pltpu.make_async_remote_copy(
-                src_ref=t_send.at[at], dst_ref=t_recv.at[slot], send_sem=t_ss.at[at],
-                recv_sem=t_rs.at[slot], device_id={"cell": d}, device_id_type=MESH)
+                src_ref=t_send.at[at], dst_ref=t_recv.at[relay], send_sem=t_ss.at[at],
+                recv_sem=t_rs.at[relay], device_id={"cell": d}, device_id_type=MESH)
+
+        def m_copy(at):
+            return pltpu.make_async_remote_copy(
+                src_ref=t_send.at[at], dst_ref=t_mid.at[at], send_sem=t_ss.at[at],
+                recv_sem=m_rs.at[at], device_id={"cell": 1}, device_id_type=MESH)
 
         for at, d in reversed(list(enumerate(trunk_dests))):
             @pl.when(trunk_need(d, s))
@@ -273,16 +306,34 @@
                 def _():
                     t_own[...] = total[...]
 
-                @pl.when(c != d)
+                @pl.when(c == 1)
+                def _():
+                    t_relay[at] = total[...]
+
+                @pl.when((c != d) & (c != 1))
                 def _():
                     t_send[at] = total[...].astype(BF16)
-                    t_copy(at, d).start()
-
-        for copy in z_copies:
-            copy.wait()
-        d_copies = [to_scen(dc.at[s], dc.at[s], d_ss, d_rs, k) for k in range(1, scens)]
-        for copy in d_copies:
-            copy.start()
+
+                @pl.when((c != d) & (c > 1))
+                def _():
+                    t_copy(at, d, 0).start()
+
+                @pl.when(c == 0)
+                def _():
+                    m_copy(at).start()
+
+        for k, copy in enumerate(z_copies):
+            @pl.when(takes_dc)
+            def _():
+                copy.wait_recv()
+                for other in share(k + 1):
+                    other.start()
+
+        for j in range(cells):
+            @pl.when(takes_dc)
+            def _():
+                share(j)[0].wait_recv()
+                pass_on(j).start()
 
         has_in = first < in_rows
         has_hid = (first + own_rows > in_rows) & (first < branch_rows)
@@ -304,9 +355,19 @@
             pick_hid[...] = contract(choose(pad_rows, bwidth, first, 1, in_rows),
                                      hid_whole[...], 1, 1).astype(BF16)
 
+        for at, d in reversed(list(enumerate(trunk_dests))):
+            @pl.when(trunk_need(d, s) & (c == 1))
+            def _():
+                m_copy(at).wait_recv()
+                t_send[at] = (t_relay[at] + t_mid[at].astype(F32)).astype(BF16)
+                t_copy(at, d, 1).start()
+
         total[...] = jnp.zeros_like(total)
-        for copy in d_copies:
-            copy.wait()
+        @pl.when(takes_dc)
+        def _():
+            for j in range(cells):
+                share(j)[1].wait_recv()
+                pass_on(j).wait_recv()
         dc_whole = dc.reshape(all_scen, WIDE)
 
         @pl.when(has_hid)
@@ -327,20 +388,28 @@
         @pl.when(has_trunk)
         def _():
             total[...] += t_own[...]
-            for k in range(cells - 1):
-                pltpu.make_async_remote_copy(
-                    src_ref=t_send.at[0], dst_ref=t_recv.at[k], send_sem=t_ss.at[0],
-                    recv_sem=t_rs.at[k], device_id={"cell": cell_at(1)},
-                    device_id_type=MESH).wait_recv()
+            for k in range(2):
+                t_copy(0, 0, k).wait_recv()
                 total[...] += t_recv[k].astype(F32)
 
         for j in range(WIDE // 128):
             out[pl.ds(j, own_rows, WIDE // 128), :] = total[0:own_rows, j * 128:(j + 1) * 128]
 
+        for k, copy in enumerate(z_copies):
+            @pl.when(cell_at(k + 1) < branch_cells)
+            def _():
+                copy.wait_send()
+
+        @pl.when(takes_dc)
+        def _():
+            for j in range(cells):
+                for copy in share(j) + [pass_on(j)]:
+                    copy.wait_send()
+
         for at, d in enumerate(trunk_dests):
             @pl.when(trunk_need(d, s) & (c != d))
             def _():
-                t_copy(at, d).wait_send()
+                t_copy(at, d, 0).wait_send()
 
     dma = pltpu.SemaphoreType.DMA
     scratch = [
@@ -371,15 +440,19 @@
         pltpu.VMEM((pad_rows, all_scen), BF16),
         pltpu.VMEM((pad_rows, WIDE), F32),
         pltpu.VMEM((len(trunk_dests), pad_rows, WIDE), BF16),
-        pltpu.VMEM((cells - 1, pad_rows, WIDE), BF16),
+        pltpu.VMEM((2, pad_rows, WIDE), BF16),
+        pltpu.VMEM((len(trunk_dests), pad_rows, WIDE), BF16),
+        pltpu.VMEM((len(trunk_dests), pad_rows, WIDE), F32),
         pltpu.VMEM((all_scen, bwidth), BF16),
         pltpu.VMEM((pad_rows, WIDE), F32),
         dma((scens - 1,)), dma((scens - 1,)),
         dma((scens - 1,)), dma((scens - 1,)),
         dma((cells - 1,)), dma((cells - 1,)),
         dma((cells - 1,)), dma((cells - 1,)),
-        dma((scens - 1,)), dma((scens - 1,)),
-        dma((len(trunk_dests),)), dma((cells - 1,)),
+        dma((cells,)), dma((cells,)),
+        dma((cells,)), dma((cells,)),
+        dma((cells,)), dma((cells,)),
+        dma((len(trunk_dests),)), dma((2,)), dma((len(trunk_dests),)),
     ]
     return kernel, scratch
 
@@ -396,12 +469,12 @@
     size = (samples + groups + width) * bwidth + (feats + classes + width) * twidth
     block = size // (cells * scens)
     fits = (
-        cells > 1 and scens > 1 and width == WIDE and twidth == WIDE and bwidth == 2 * WIDE
+        cells == 4 and scens == 4 and width == WIDE and twidth == WIDE and bwidth == 2 * WIDE
         and block % WIDE == 0 and block * cells * scens == size
         and scen_rows == 128 and scen_rows % (16 * cells) == 0 and cell_rows % 128 == 0
         and samples == 128 and feats == 128 and groups <= 128 and classes <= 128
         and groups % 16 == 0 and classes % 16 == 0 and scens * scen_rows <= 1024
-        and cell_rows <= 512
+        and cell_rows <= 512 and (samples + groups) * 2 + bwidth >= 2 * scens * (block // WIDE)
     )
     if not fits:
         return plain_shards(hydrograph, scen_group, cell_feat, cell_class, branch_in, group_table,

time: 30.7 us -> 28.8 us (0.938)
  the two profiles are of different devices: /device:TPU:1 before, /device:TPU:18 now
where the time goes in v3:
time: 28.8 us; the launch traced here: 28.6 us
  Pallas kernels  26.9 us (93%)
  local copies, waits for them, and re-layouts  1.66 us (6%)
    pallas_call x1, Pallas kernels, shards(): pl.pallas_call(kernel, out_shape=jax.ShapeDtypeStruct((block // 128, 128)...  26.9 us
    unnamed x1, local copies, waits for them, and re-layouts  1.66 us

profile of v3, /device:TPU:18, one launch (start us, length us, event | category | flops | bytes accessed | tf_op | source)
XLA Modules:
  0.0 28.6 jit_solution(3400784992682682090)
XLA Ops:
  0.0 26.9 %shard_map.109 = f32[492,128]{1,0:T(8,128)} custom-call(bf16[128,128]{1,0:T(8,128)(2,1)} %hydro.1, s32[1,128]{1,0:T(1,128)} %bitcast.3, bf16[512,128]{1,0:T(8,128)(2,1)} %feat.1, s32[4]{0:T(128)} %klass_h.1, bf16[128,1024]{1,0:T(8,128)(2,1)} %b_in.1, bf16[16,1024]{1,0:T(8,128)(2,1)} %g_tab.1, bf16[1024,512]{1,0:T(8,128)(2,1)} %b_out_h.1, ...), custom_call_target="tpu_custom_call" | custom-call | tf_op jit(solution)/shard_map/pallas_call | solution.py:487
  27.0 1.7 %copy.13 = f32[62976]{0:T(1024)} copy(f32[62976]{0:T(1024)} %bitcast.2) | data formatting | bytes 503808

commit v4 on v3

--- a/solution.py
+++ b/solution.py
@@ -84,7 +84,7 @@
 
 def make_kernel(cells, scens, scen_rows, cell_rows, bwidth, twidth, groups, classes, samples, feats,
                 own_rows, pairs):
-    pad_rows = -(-own_rows // 16) * 16
+    pad_rows = -(-own_rows // 32) * 32
     chunk = scen_rows // cells
     in_rows = 2 * (samples + groups)
     branch_rows = in_rows + bwidth
@@ -96,14 +96,16 @@
         d for d in range(cells) if ((d + 1) * scens) * own_rows > branch_rows
     ]
     tile = 128
+    piece = 32
+    pieces = pad_rows // piece
     branch_cells = -(-branch_rows // (scens * own_rows))
 
     def kernel(hydro, group_h, feat, klass_h, b_in, g_tab, b_out_h, t_in, c_tab, t_out_h,
                targets_h, out,
-               group, klass, b_out, t_out, targets, in_sem, x_all, w_b, w_t, x_t, dgelu, hid, coeff, hid_t, basis, resid, part_f, part_b,
-               part_in, dc, dbasis, dpre_t, pick_in0, pick_in1, pick_hid, t_own, t_send, t_recv, t_mid, t_relay,
+               group, klass, b_out, t_out, targets, in_sem, x_all, w_b, w_t, x_t, dgelu, hid, coeff, hid_t, dtanh, basis, resid, part_f, part_b,
+               part_in, dc, dbasis, dpre_t, pick_t, pick_x, pick_in0, pick_in1, pick_hid, t_own, t_send, t_recv, t_mid, t_relay,
                dpre_b, total,
-               x_ss, x_rs, r_ss, r_rs, p_ss, p_rs, z_ss, z_rs, f_ss, f_rs, n_ss, n_rs, g_ss, g_rs, t_ss, t_rs, m_rs):
+               x_ss, x_rs, i_ss, i_rs, r_ss, r_rs, p_ss, p_rs, z_ss, z_rs, f_ss, f_rs, n_ss, n_rs, g_ss, g_rs, t_ss, t_rs, m_rs):
         c = lax.axis_index("cell")
         s = lax.axis_index("scen")
         first = (c * scens + s) * own_rows
@@ -135,7 +137,7 @@
         loads = [
             pltpu.make_async_copy(src, dst, in_sem.at[at])
             for at, (src, dst) in enumerate([
-                (group_h, group),
+                (group_h, group.at[s]),
                 (hydro, x_all.at[s, :, 0:samples]),
                 (b_in, w_b.at[0:samples]),
                 (g_tab, w_b.at[samples:samples + groups]),
@@ -156,12 +158,10 @@
         for k in range(1, cells):
             pl.semaphore_signal(barrier, inc=1, device_id={"cell": cell_at(k)}, device_id_type=MESH)
 
-        loads[0].wait()
-        loads[1].wait()
-        hot = (lax.broadcasted_iota(jnp.int32, (128, scen_rows), 0) == group[...]).astype(F32)
-        x_all[s, :, samples:samples + 128] = hot.T.astype(BF16)
         pl.semaphore_wait(barrier, scens + cells - 2)
-        x_copies = [to_scen(x_all.at[s], x_all.at[s], x_ss, x_rs, k) for k in range(1, scens)]
+        x_copies = [to_scen(hydro, x_all.at[s, :, 0:samples], x_ss, x_rs, k)
+                    for k in range(1, scens)]
+        x_copies += [to_scen(group_h, group.at[s], i_ss, i_rs, k) for k in range(1, scens)]
         for copy in x_copies:
             copy.start()
 
@@ -169,6 +169,8 @@
         w_t[feats + classes:, :] = jnp.zeros((128 - classes, twidth), BF16)
 
         def branch(p):
+            hot = (lax.broadcasted_iota(jnp.int32, (128, scen_rows), 0) == group[p]).astype(F32)
+            x_all[p, :, samples:samples + 128] = hot.T.astype(BF16)
             pre = contract(x_all[p], w_b[...], 1, 0)
             inner = math.sqrt(2.0 / math.pi)
             bent = jnp.tanh(inner * (pre + 0.044715 * (pre * pre * pre)))
@@ -178,7 +180,7 @@
                 1.0 + (3.0 * 0.044715) * (pre * pre))
             coeff[p] = contract(hid[p], b_out[...], 1, 0).astype(BF16)
 
-        for load in loads[2:5]:
+        for load in loads[0:5]:
             load.wait()
         branch(s)
         for load in loads[5:10]:
@@ -190,7 +192,9 @@
             lane = lax.broadcasted_iota(jnp.int32, (tile, 128), 1)
             x_t[rows, feats:feats + 128] = (lane == klass[b]).astype(F32).astype(BF16)
             pre = contract(x_t[rows, :], w_t[...], 1, 0)
-            hid_t[rows, :] = jnp.tanh(pre).astype(BF16)
+            bent = jnp.tanh(pre)
+            hid_t[rows, :] = bent.astype(BF16)
+            dtanh[rows, :] = 1.0 - bent * bent
             basis[rows, :] = contract(hid_t[rows, :], t_out[...], 1, 0).astype(BF16)
 
         loads[10].wait()
@@ -209,11 +213,58 @@
         for copy in p_copies:
             copy.start()
 
+        def trunk_need(d, me):
+            return (d * scens + me + 1) * own_rows > branch_rows
+
+        def lead_need(d, me):
+            return ((d * scens + me + 1) * own_rows > branch_rows) & (
+                (d * scens + me) * own_rows < branch_rows + trunk_lead)
+
+        lead_any = lead_need(trunk_dests[0], s)
+        for d in trunk_dests[1:]:
+            lead_any = lead_any | lead_need(d, s)
+
+        for at, d in enumerate(trunk_dests):
+            base = (d * scens + s) * own_rows
+
+            @pl.when(trunk_need(d, s))
+            def _():
+                pick_t[at] = contract(
+                    choose(pad_rows, twidth, base, 1, branch_rows + trunk_lead), hid_t[...], 1, 1
+                ).astype(BF16)
+
+            @pl.when(lead_need(d, s))
+            def _():
+                keep = (lax.broadcasted_iota(jnp.int32, (pad_rows, feats + 128), 1)
+                        < trunk_lead).astype(F32).astype(BF16)
+                pick_x[at] = contract(choose(pad_rows, feats + 128, base, 1, branch_rows) * keep,
+                                      x_t[...], 1, 1).astype(BF16)
+
         for copy in x_copies:
             copy.wait()
         @pl.loop(1, scens)
         def _(k):
             branch(lax.rem(s + k, scens))
+
+        has_in = first < in_rows
+        has_hid = (first + own_rows > in_rows) & (first < branch_rows)
+        has_trunk = first + own_rows > branch_rows
+        x_whole = x_all.reshape(all_scen, samples + 128)
+        hid_whole = hid.reshape(all_scen, bwidth)
+
+        @pl.when(has_in)
+        def _():
+            keep = (lax.broadcasted_iota(jnp.int32, (pad_rows, samples + 128), 1)
+                    < samples + groups).astype(F32).astype(BF16)
+            pick_in0[...] = contract(choose(pad_rows, samples + 128, first, 2, 0) * keep,
+                                     x_whole[...], 1, 1).astype(BF16)
+            pick_in1[...] = contract(choose(pad_rows, samples + 128, first, 2, 1) * keep,
+                                     x_whole[...], 1, 1).astype(BF16)
+
+        @pl.when(has_hid)
+        def _():
+            pick_hid[...] = contract(choose(pad_rows, bwidth, first, 1, in_rows),
+                                     hid_whole[...], 1, 1).astype(BF16)
 
         r_far.wait()
         r_pass = to_peer(resid.at[far], r_ss, r_rs, 2, sibling)
@@ -254,53 +305,40 @@
                 sums = sums + contract(resid[p, :, cols], coeff[p], 0, 0)
             dbasis[cols, :] = sums.astype(BF16)
 
-        def trunk_need(d, me):
-            return (d * scens + me + 1) * own_rows > branch_rows
-
-        def lead_need(d, me):
-            return ((d * scens + me + 1) * own_rows > branch_rows) & (
-                (d * scens + me) * own_rows < branch_rows + trunk_lead)
-
-        lead_any = lead_need(trunk_dests[0], s)
-        for d in trunk_dests[1:]:
-            lead_any = lead_any | lead_need(d, s)
-
         @pl.when(lead_any)
         def _():
             @pl.loop(0, cell_rows // tile)
             def _(b):
                 rows = pl.ds(pl.multiple_of(b * tile, tile), tile)
-                h = contract(x_t[rows, :], w_t[...], 1, 0)
-                h = jnp.tanh(h)
                 d_hid = contract(dbasis[rows, :], t_out[...], 1, 1)
-                dpre_t[rows, :] = ((1.0 - h * h) * d_hid).astype(BF16)
-
-        def t_copy(at, d, relay):
+                dpre_t[rows, :] = (dtanh[rows, :] * d_hid).astype(BF16)
+
+        def rows_of(j):
+            return pl.ds(j * piece, piece)
+
+        def t_copy(at, d, relay, j):
             return pltpu.make_async_remote_copy(
-                src_ref=t_send.at[at], dst_ref=t_recv.at[relay], send_sem=t_ss.at[at],
-                recv_sem=t_rs.at[relay], device_id={"cell": d}, device_id_type=MESH)
-
-        def m_copy(at):
+                src_ref=t_send.at[at, rows_of(j)], dst_ref=t_recv.at[relay, rows_of(j)],
+                send_sem=t_ss.at[at, j], recv_sem=t_rs.at[relay, j], device_id={"cell": d},
+                device_id_type=MESH)
+
+        def m_copy(at, j):
             return pltpu.make_async_remote_copy(
-                src_ref=t_send.at[at], dst_ref=t_mid.at[at], send_sem=t_ss.at[at],
-                recv_sem=m_rs.at[at], device_id={"cell": 1}, device_id_type=MESH)
+                src_ref=t_send.at[at, rows_of(j)], dst_ref=t_mid.at[at, rows_of(j)],
+                send_sem=t_ss.at[at, j], recv_sem=m_rs.at[at, j], device_id={"cell": 1},
+                device_id_type=MESH)
+
+        def piece_need(d, j):
+            return (d * scens + s) * own_rows + min((j + 1) * piece, own_rows) > branch_rows
 
         for at, d in reversed(list(enumerate(trunk_dests))):
             @pl.when(trunk_need(d, s))
             def _():
-                base = (d * scens + s) * own_rows
-                pick = contract(
-                    choose(pad_rows, twidth, base, 1, branch_rows + trunk_lead), hid_t[...], 1, 1)
-                total[...] = contract(pick.astype(BF16), dbasis[...], 1, 0)
+                total[...] = contract(pick_t[at], dbasis[...], 1, 0)
 
                 @pl.when(lead_need(d, s))
                 def _():
-                    pick = contract(
-                        choose(pad_rows, feats + 128, base, 1, branch_rows)
-                        * (lax.broadcasted_iota(jnp.int32, (pad_rows, feats + 128), 1)
-                           < trunk_lead).astype(F32).astype(BF16),
-                        x_t[...], 1, 1)
-                    total[...] += contract(pick.astype(BF16), dpre_t[...], 1, 0)
+                    total[...] += contract(pick_x[at], dpre_t[...], 1, 0)
 
                 @pl.when(c == d)
                 def _():
@@ -314,13 +352,14 @@
                 def _():
                     t_send[at] = total[...].astype(BF16)
 
-                @pl.when((c != d) & (c > 1))
-                def _():
-                    t_copy(at, d, 0).start()
-
-                @pl.when(c == 0)
-                def _():
-                    m_copy(at).start()
+                for j in range(pieces):
+                    @pl.when((c != d) & (c > 1) & piece_need(d, j))
+                    def _():
+                        t_copy(at, d, 0, j).start()
+
+                    @pl.when((c == 0) & piece_need(d, j))
+                    def _():
+                        m_copy(at, j).start()
 
         for k, copy in enumerate(z_copies):
             @pl.when(takes_dc)
@@ -335,62 +374,59 @@
                 share(j)[0].wait_recv()
                 pass_on(j).start()
 
-        has_in = first < in_rows
-        has_hid = (first + own_rows > in_rows) & (first < branch_rows)
-        has_trunk = first + own_rows > branch_rows
-        x_whole = x_all.reshape(all_scen, samples + 128)
-        hid_whole = hid.reshape(all_scen, bwidth)
-
-        @pl.when(has_in)
-        def _():
-            keep = (lax.broadcasted_iota(jnp.int32, (pad_rows, samples + 128), 1)
-                    < samples + groups).astype(F32).astype(BF16)
-            pick_in0[...] = contract(choose(pad_rows, samples + 128, first, 2, 0) * keep,
-                                     x_whole[...], 1, 1).astype(BF16)
-            pick_in1[...] = contract(choose(pad_rows, samples + 128, first, 2, 1) * keep,
-                                     x_whole[...], 1, 1).astype(BF16)
-
-        @pl.when(has_hid)
-        def _():
-            pick_hid[...] = contract(choose(pad_rows, bwidth, first, 1, in_rows),
-                                     hid_whole[...], 1, 1).astype(BF16)
-
         for at, d in reversed(list(enumerate(trunk_dests))):
-            @pl.when(trunk_need(d, s) & (c == 1))
-            def _():
-                m_copy(at).wait_recv()
-                t_send[at] = (t_relay[at] + t_mid[at].astype(F32)).astype(BF16)
-                t_copy(at, d, 1).start()
-
-        total[...] = jnp.zeros_like(total)
-        @pl.when(takes_dc)
-        def _():
-            for j in range(cells):
-                share(j)[1].wait_recv()
-                pass_on(j).wait_recv()
-        dc_whole = dc.reshape(all_scen, WIDE)
-
-        @pl.when(has_hid)
-        def _():
-            total[...] += contract(pick_hid[...], dc_whole[...], 1, 0)
-
-        @pl.when(has_in)
-        def _():
-            dc_rows = dc.reshape(scens, scen_rows, WIDE)
-            @pl.loop(0, scens)
-            def _(p):
+            for j in range(pieces):
+                @pl.when((c == 1) & piece_need(d, j))
+                def _():
+                    m_copy(at, j).wait_recv()
+                    t_send[at, rows_of(j)] = (
+                        t_relay[at, rows_of(j)] + t_mid[at, rows_of(j)].astype(F32)).astype(BF16)
+                    t_copy(at, d, 1, j).start()
+
+        dc_rows = dc.reshape(scens, scen_rows, WIDE)
+
+        def through_gelu(p):
+            @pl.when(has_in)
+            def _():
                 d_hid = contract(dc_rows[p], b_out[...], 1, 1)
                 rows = pl.ds(pl.multiple_of(p * scen_rows, scen_rows), scen_rows)
                 dpre_b[rows, :] = (d_hid * dgelu[p]).astype(BF16)
+
+        total[...] = jnp.zeros_like(total)
+        through_gelu(s)
+        through_gelu(far)
+
+        @pl.when(takes_dc)
+        def _():
+            for j in range(cells):
+                share(j)[1].wait_recv()
+        through_gelu(sibling)
+
+        @pl.when(takes_dc)
+        def _():
+            for j in range(cells):
+                pass_on(j).wait_recv()
+        through_gelu(lax.rem(sibling + scens // 2, scens))
+        dc_whole = dc.reshape(all_scen, WIDE)
+
+        @pl.when(has_hid)
+        def _():
+            total[...] += contract(pick_hid[...], dc_whole[...], 1, 0)
+
+        @pl.when(has_in)
+        def _():
             total[...] += contract(pick_in0[...], dpre_b[:, :WIDE], 1, 0)
             total[...] += contract(pick_in1[...], dpre_b[:, WIDE:], 1, 0)
 
         @pl.when(has_trunk)
         def _():
             total[...] += t_own[...]
-            for k in range(2):
-                t_copy(0, 0, k).wait_recv()
-                total[...] += t_recv[k].astype(F32)
+            for j in range(pieces):
+                @pl.when(first + min((j + 1) * piece, own_rows) > branch_rows)
+                def _():
+                    for k in range(2):
+                        t_copy(0, 0, k, j).wait_recv()
+                        total[rows_of(j)] += t_recv[k, rows_of(j)].astype(F32)
 
         for j in range(WIDE // 128):
             out[pl.ds(j, own_rows, WIDE // 128), :] = total[0:own_rows, j * 128:(j + 1) * 128]
@@ -407,13 +443,14 @@
                     copy.wait_send()
 
         for at, d in enumerate(trunk_dests):
-            @pl.when(trunk_need(d, s) & (c != d))
-            def _():
-                t_copy(at, d, 0).wait_send()
+            for j in range(pieces):
+                @pl.when((c != d) & piece_need(d, j))
+                def _():
+                    t_copy(at, d, 0, j).wait_send()
 
     dma = pltpu.SemaphoreType.DMA
     scratch = [
-        pltpu.VMEM((1, scen_rows), jnp.int32),
+        pltpu.VMEM((scens, 1, scen_rows), jnp.int32),
         pltpu.SMEM((cell_rows // 128,), jnp.int32),
         pltpu.VMEM((bwidth, WIDE), BF16),
         pltpu.VMEM((twidth, WIDE), BF16),
@@ -427,6 +464,7 @@
         pltpu.VMEM((scens, scen_rows, bwidth), BF16),
         pltpu.VMEM((scens, scen_rows, WIDE), BF16),
         pltpu.VMEM((cell_rows, twidth), BF16),
+        pltpu.VMEM((cell_rows, twidth), F32),
         pltpu.VMEM((cell_rows, WIDE), BF16),
         pltpu.VMEM((scens, scen_rows, cell_rows), BF16),
         pltpu.VMEM((cells, chunk, WIDE), F32),
@@ -435,6 +473,8 @@
         pltpu.VMEM((scens, cells, chunk, WIDE), BF16),
         pltpu.VMEM((cell_rows, WIDE), BF16),
         pltpu.VMEM((cell_rows, twidth), BF16),
+        pltpu.VMEM((len(trunk_dests), pad_rows, cell_rows), BF16),
+        pltpu.VMEM((len(trunk_dests), pad_rows, cell_rows), BF16),
         pltpu.VMEM((pad_rows, all_scen), BF16),
         pltpu.VMEM((pad_rows, all_scen), BF16),
         pltpu.VMEM((pad_rows, all_scen), BF16),
@@ -447,12 +487,13 @@
         pltpu.VMEM((pad_rows, WIDE), F32),
         dma((scens - 1,)), dma((scens - 1,)),
         dma((scens - 1,)), dma((scens - 1,)),
+        dma((scens - 1,)), dma((scens - 1,)),
         dma((cells - 1,)), dma((cells - 1,)),
         dma((cells - 1,)), dma((cells - 1,)),
         dma((cells,)), dma((cells,)),
         dma((cells,)), dma((cells,)),
         dma((cells,)), dma((cells,)),
-        dma((len(trunk_dests),)), dma((2,)), dma((len(trunk_dests),)),
+        dma((len(trunk_dests), pieces)), dma((2, pieces)), dma((len(trunk_dests), pieces)),
     ]
     return kernel, scratch
 

time: 28.8 us -> 26.8 us (0.931)
  the two profiles are of different devices: /device:TPU:18 before, /device:TPU:19 now
where the time goes in v4:
time: 26.8 us; the launch traced here: 26.7 us
  Pallas kernels  25 us (93%)
  local copies, waits for them, and re-layouts  1.66 us (6%)
    pallas_call x1, Pallas kernels, shards(): pl.pallas_call(kernel, out_shape=jax.ShapeDtypeStruct((block // 128, 128)...  25 us
    unnamed x1, local copies, waits for them, and re-layouts  1.66 us

profile of v4, /device:TPU:19, one launch (start us, length us, event | category | flops | bytes accessed | tf_op | source)
XLA Modules:
  0.0 26.7 jit_solution(17439482001221344517)
XLA Ops:
  0.0 25.0 %shard_map.109 = f32[492,128]{1,0:T(8,128)} custom-call(bf16[128,128]{1,0:T(8,128)(2,1)} %hydro.1, s32[1,128]{1,0:T(1,128)} %bitcast.3, bf16[512,128]{1,0:T(8,128)(2,1)} %feat.1, s32[4]{0:T(128)} %klass_h.1, bf16[128,1024]{1,0:T(8,128)(2,1)} %b_in.1, bf16[16,1024]{1,0:T(8,128)(2,1)} %g_tab.1, bf16[1024,512]{1,0:T(8,128)(2,1)} %b_out_h.1, ...), custom_call_target="tpu_custom_call" | custom-call | tf_op jit(solution)/shard_map/pallas_call | solution.py:528
  25.0 1.7 %copy.13 = f32[62976]{0:T(1024)} copy(f32[62976]{0:T(1024)} %bitcast.2) | data formatting | bytes 503808

commit v5 on v4

--- a/solution.py
+++ b/solution.py
@@ -246,26 +246,6 @@
         def _(k):
             branch(lax.rem(s + k, scens))
 
-        has_in = first < in_rows
-        has_hid = (first + own_rows > in_rows) & (first < branch_rows)
-        has_trunk = first + own_rows > branch_rows
-        x_whole = x_all.reshape(all_scen, samples + 128)
-        hid_whole = hid.reshape(all_scen, bwidth)
-
-        @pl.when(has_in)
-        def _():
-            keep = (lax.broadcasted_iota(jnp.int32, (pad_rows, samples + 128), 1)
-                    < samples + groups).astype(F32).astype(BF16)
-            pick_in0[...] = contract(choose(pad_rows, samples + 128, first, 2, 0) * keep,
-                                     x_whole[...], 1, 1).astype(BF16)
-            pick_in1[...] = contract(choose(pad_rows, samples + 128, first, 2, 1) * keep,
-                                     x_whole[...], 1, 1).astype(BF16)
-
-        @pl.when(has_hid)
-        def _():
-            pick_hid[...] = contract(choose(pad_rows, bwidth, first, 1, in_rows),
-                                     hid_whole[...], 1, 1).astype(BF16)
-
         r_far.wait()
         r_pass = to_peer(resid.at[far], r_ss, r_rs, 2, sibling)
         r_pass.start()
@@ -294,6 +274,26 @@
         def _():
             for copy in share(0):
                 copy.start()
+
+        has_in = first < in_rows
+        has_hid = (first + own_rows > in_rows) & (first < branch_rows)
+        has_trunk = first + own_rows > branch_rows
+        x_whole = x_all.reshape(all_scen, samples + 128)
+        hid_whole = hid.reshape(all_scen, bwidth)
+
+        @pl.when(has_in)
+        def _():
+            keep = (lax.broadcasted_iota(jnp.int32, (pad_rows, samples + 128), 1)
+                    < samples + groups).astype(F32).astype(BF16)
+            pick_in0[...] = contract(choose(pad_rows, samples + 128, first, 2, 0) * keep,
+                                     x_whole[...], 1, 1).astype(BF16)
+            pick_in1[...] = contract(choose(pad_rows, samples + 128, first, 2, 1) * keep,
+                                     x_whole[...], 1, 1).astype(BF16)
+
+        @pl.when(has_hid)
+        def _():
+            pick_hid[...] = contract(choose(pad_rows, bwidth, first, 1, in_rows),
+                                     hid_whole[...], 1, 1).astype(BF16)
 
         r_near.wait()
         r_pass.wait()

time: 26.8 us -> 26.6 us (level)
  the two profiles are of different devices: /device:TPU:19 before, /device:TPU:23 now
where the time goes in v5:
time: 26.6 us; the launch traced here: 26.4 us
  Pallas kernels  24.8 us (93%)
  local copies, waits for them, and re-layouts  1.66 us (6%)
    pallas_call x1, Pallas kernels, shards(): pl.pallas_call(kernel, out_shape=jax.ShapeDtypeStruct((block // 128, 128)...  24.8 us
    unnamed x1, local copies, waits for them, and re-layouts  1.66 us

profile of v5, /device:TPU:23, one launch (start us, length us, event | category | flops | bytes accessed | tf_op | source)
XLA Modules:
  0.0 26.4 jit_solution(5512226936655844751)
XLA Ops:
  0.0 24.8 %shard_map.109 = f32[492,128]{1,0:T(8,128)} custom-call(bf16[128,128]{1,0:T(8,128)(2,1)} %hydro.1, s32[1,128]{1,0:T(1,128)} %bitcast.3, bf16[512,128]{1,0:T(8,128)(2,1)} %feat.1, s32[4]{0:T(128)} %klass_h.1, bf16[128,1024]{1,0:T(8,128)(2,1)} %b_in.1, bf16[16,1024]{1,0:T(8,128)(2,1)} %g_tab.1, bf16[1024,512]{1,0:T(8,128)(2,1)} %b_out_h.1, ...), custom_call_target="tpu_custom_call" | custom-call | tf_op jit(solution)/shard_map/pallas_call | solution.py:528
  24.8 1.7 %copy.13 = f32[62976]{0:T(1024)} copy(f32[62976]{0:T(1024)} %bitcast.2) | data formatting | bytes 503808
